TPU v7x, 32 devices: a whole 2x2x4 slice. The times are simulated.
32 devices in a mesh: gx: 4 (over y, x), gy: 2 (over core), gz: 4 (over z).
Axes of the slice: x: 2, y: 2, z: 4, core: 2. Of those that a mesh axis runs over, the one named last changes fastest.
Arguments:
- conductance: float32 [64, 64, 512], P('gx', 'gy', 'gz'), may hold values from 0.1 to 1
- reaction: float32 [64, 64, 512], P('gx', 'gy', 'gz'), may hold values from 0.1 to 1
- source: float32 [64, 64, 512], P('gx', 'gy', 'gz'), may hold values from -8 to 8
Outputs:
- pressure: float32 [64, 64, 512], P('gx', 'gy', 'gz')
- residual: float32 [64, 64, 512], P('gx', 'gy', 'gz')
All inputs are finite; a program needn't handle non-finite values.
Results may differ from a plain program's by a relative error of at most 0.0003.
Values sent between devices are 32-bit elements; how exact they have to be, the bound alone decides.
A program may use at most 64 MiB of HBM per device.

v0:
```python
import jax
import jax.numpy as jnp
from jax import lax
from jax.sharding import PartitionSpec as P

ITERS = 3


chebyshev_low = 0.15
chebyshev_high = 2.0
chebyshev_mid = 0.5 * (chebyshev_high + chebyshev_low)
chebyshev_half = 0.5 * (chebyshev_high - chebyshev_low)
chebyshev_ratio = chebyshev_mid / chebyshev_half
rho_first = 1.0 / chebyshev_ratio
rho_second = 1.0 / (2.0 * chebyshev_ratio - rho_first)
rho_third = 1.0 / (2.0 * chebyshev_ratio - rho_second)
first_scale = 1.0 / chebyshev_mid
keep_second = rho_second * rho_first
push_second = 2.0 * rho_second / chebyshev_half
keep_third = rho_third * rho_second
push_third = 2.0 * rho_third / chebyshev_half


def padded_2(cells, sides, width):
    for axis, dim in sides:
        count = lax.axis_size(axis)
        ends = count - 1
        head = lax.slice_in_dim(cells, 0, width, axis=dim)
        tail = lax.slice_in_dim(cells, cells.shape[dim] - width, cells.shape[dim], axis=dim)
        cells = jnp.concatenate(
            [
                lax.ppermute(tail, axis, [(i, (i + 1) % count) for i in range(ends)]),
                cells,
                lax.ppermute(head, axis, [((i + 1) % count, i) for i in range(ends)]),
            ],
            axis=dim,
        )
    return cells


def harmonic(lower_cell, upper_cell):
    summed = lower_cell + upper_cell
    return 2.0 * lower_cell * upper_cell / jnp.where(summed > 0.0, summed, 1.0)


def face_terms(padded, shift_term):
    centre = padded[1:-1, 1:-1, 1:-1]
    uppers = (
        harmonic(centre, padded[2:, 1:-1, 1:-1]),
        harmonic(centre, padded[1:-1, 2:, 1:-1]),
        harmonic(centre, padded[1:-1, 1:-1, 2:]),
    )
    lowers = (
        harmonic(centre, padded[:-2, 1:-1, 1:-1]),
        harmonic(centre, padded[1:-1, :-2, 1:-1]),
        harmonic(centre, padded[1:-1, 1:-1, :-2]),
    )
    diagonal = shift_term + uppers[0] + lowers[0] + uppers[1] + lowers[1] + uppers[2] + lowers[2]
    return (uppers, lowers, diagonal)


def stencil(padded, operator_terms):
    uppers, lowers, diagonal = operator_terms
    result = diagonal * padded[1:-1, 1:-1, 1:-1]
    result = result - uppers[0] * padded[2:, 1:-1, 1:-1] - lowers[0] * padded[:-2, 1:-1, 1:-1]
    result = result - uppers[1] * padded[1:-1, 2:, 1:-1] - lowers[1] * padded[1:-1, :-2, 1:-1]
    result = result - uppers[2] * padded[1:-1, 1:-1, 2:] - lowers[2] * padded[1:-1, 1:-1, :-2]
    return result


def interior(array, depth):
    return array[depth:-depth, depth:-depth, depth:-depth]


def trim_terms(operator_terms, depth):
    uppers, lowers, diagonal = operator_terms
    return (
        tuple((interior(member, depth) for member in uppers)),
        tuple((interior(member, depth) for member in lowers)),
        interior(diagonal, depth),
    )


def shards(conductance, reaction, source):
    stacked = jnp.stack((conductance, reaction), 0)
    cell_halo = padded_2(stacked, (("gx", 1), ("gy", 2), ("gz", 3)), 4)
    wide_terms = face_terms(cell_halo[0], interior(cell_halo[1], 1))
    inside = (interior(cell_halo[0], 1) > 0.0).astype(jnp.float32)
    wide_inverse = inside / (wide_terms[2] + (1.0 - inside))
    outer_terms = trim_terms(wide_terms, 1)
    middle_terms = trim_terms(wide_terms, 2)
    own_terms = trim_terms(wide_terms, 3)
    outer_inverse = interior(wide_inverse, 1)
    middle_inverse = interior(wide_inverse, 2)

    def apply_both(vector):
        widened = padded_2(vector, (("gx", 0), ("gy", 1), ("gz", 2)), 3)
        update = wide_inverse * widened * first_scale
        approx = update
        residue = interior(widened, 1) - stencil(approx, outer_terms)
        update = keep_second * interior(update, 1) + push_second * (outer_inverse * residue)
        approx = interior(approx, 1) + update
        residue = interior(widened, 2) - stencil(approx, middle_terms)
        update = keep_third * interior(update, 1) + push_third * (middle_inverse * residue)
        result_cycle = interior(approx, 1) + update
        return (interior(result_cycle, 1), stencil(result_cycle, own_terms))

    pressure = jnp.zeros_like(source)
    residual = source
    u_vec, w_vec = apply_both(residual)
    z_dir = jnp.zeros_like(source)
    q_dir = jnp.zeros_like(source)
    s_dir = jnp.zeros_like(source)
    p_dir = jnp.zeros_like(source)
    gamma_prev = jnp.float32(1.0)
    alpha_prev = jnp.float32(1.0)
    for iteration in range(ITERS):
        gamma_sum, curvature = lax.psum(
            (jnp.sum(residual * u_vec), jnp.sum(w_vec * u_vec)), ("gx", "gy", "gz")
        )
        m_vec, n_vec = apply_both(w_vec)
        if iteration == 0:
            step_beta = jnp.float32(0.0)
            step_alpha = gamma_sum / curvature
        else:
            step_beta = gamma_sum / gamma_prev
            step_alpha = gamma_sum / (curvature - step_beta * gamma_sum / alpha_prev)
        z_dir = n_vec + step_beta * z_dir
        q_dir = m_vec + step_beta * q_dir
        s_dir = w_vec + step_beta * s_dir
        p_dir = u_vec + step_beta * p_dir
        pressure = pressure + step_alpha * p_dir
        residual = residual - step_alpha * s_dir
        u_vec = u_vec - step_alpha * q_dir
        w_vec = w_vec - step_alpha * z_dir
        gamma_prev = gamma_sum
        alpha_prev = step_alpha
    return (pressure, residual)


def solution(mesh):
    placed = (P("gx", "gy", "gz"), P("gx", "gy", "gz"), P("gx", "gy", "gz"))
    return jax.shard_map(
        shards,
        mesh=mesh,
        in_specs=placed,
        out_specs=(P("gx", "gy", "gz"), P("gx", "gy", "gz")),
        check_vma=False,
    )
```

profile of v0, /device:TPU:0, one launch (start us, length us, event | category | flops | bytes accessed | tf_op | source)
XLA Modules:
  0.0 273.4 jit_solution(5693009224788059224)
XLA Ops:
  0.7 0.9 fusion.116
  1.5 1.3 collective-permute-start.7
  2.8 5.5 %collective-permute-start.6 = (f32[3,32,128]{2,1,0:T(8,128)S(1)}, f32[3,32,128]{2,1,0:T(8,128)S(1)}, u32[]{:S(2)}, u32[]{:S(2)}) collective-permute-start(f32[3,32,128]{2,1,0:T(8,128)S(1)} %get-tuple-element.72), channel_id=1, source_target_pairs={{0,8},{8,16},{16,24},{1,9},{9,17},{17,25},{2,10},{10,18},{18,26},{... | collective-permute-start | bytes 147464 | tf_op jit(solution)/shard_map/ppermute | solution.py:32
  8.3 1.0 pad_maximum_fusion.9
  9.3 4.8 %collective-permute-start = (f32[2,4,32,128]{3,2,1,0:T(8,128)S(1)}, f32[2,4,32,128]{3,2,1,0:T(8,128)S(1)}, u32[]{:S(2)}, u32[]{:S(2)}) collective-permute-start(f32[2,4,32,128]{3,2,1,0:T(8,128)S(1)} %get-tuple-element.53), channel_id=1, source_target_pairs={{0,8},{8,16},{16,24},{1,9},{9,17},{17,25},{2,10},{10,18},{18,26},{... | collective-permute-start | bytes 393224 | tf_op jit(solution)/shard_map/ppermute | solution.py:32
  14.1 1.3 collective-permute-start.1
  15.4 1.0 constant_dynamic-update-slice_fusion.1
  16.5 1.3 collective-permute-start.9
  17.8 3.0 %collective-permute-start.8 = (f32[22,3,128]{2,0,1:T(8,128)S(1)}, f32[22,3,128]{2,0,1:T(8,128)S(1)}, u32[]{:S(2)}, u32[]{:S(2)}) collective-permute-start(f32[22,3,128]{2,0,1:T(8,128)S(1)} %copy.114), channel_id=1, source_target_pairs={{0,4},{1,5},{2,6},{3,7},{8,12},{9,13},{10,14},{11,15},{16,20},{17,... | collective-permute-start | bytes 101384 | tf_op jit(solution)/shard_map/ppermute | solution.py:32
  20.9 0.8 collective-permute-done.8
  21.8 1.3 collective-permute-start.3
  23.1 3.0 %collective-permute-start.2 = (f32[2,24,4,128]{3,1,2,0:T(8,128)S(1)}, f32[2,24,4,128]{3,1,2,0:T(8,128)S(1)}, u32[]{:S(2)}, u32[]{:S(2)}) collective-permute-start(f32[2,24,4,128]{3,1,2,0:T(8,128)S(1)} %copy.112), channel_id=1, source_target_pairs={{0,4},{1,5},{2,6},{3,7},{8,12},{9,13},{10,14},{11,15},{16,20},{17,... | collective-permute-start | bytes 294920 | tf_op jit(solution)/shard_map/ppermute | solution.py:32
  26.3 0.8 collective-permute-done.2
  27.1 0.6 copy-done.26
  27.9 1.3 fusion.109
  29.2 1.6 copy.96
  30.8 0.4 copy.97
  31.2 1.4 collective-permute-start.5
  32.6 4.6 %collective-permute-start.4 = (f32[2,24,40,4]{2,1,3,0:T(8,128)S(1)}, f32[2,24,40,4]{2,1,3,0:T(8,128)S(1)}, u32[]{:S(2)}, u32[]{:S(2)}) collective-permute-start(f32[2,24,40,4]{2,1,3,0:T(8,128)S(1)} %copy.96), channel_id=1, source_target_pairs={{0,1},{1,2},{2,3},{4,5},{5,6},{6,7},{8,9},{9,10},{10,11},{12,13},{... | collective-permute-start | bytes 92168 | tf_op jit(solution)/shard_map/ppermute | solution.py:32
  37.2 1.0 fusion.112
  38.2 4.2 %collective-permute-start.10 = (f32[22,38,3]{2,1,0:T(8,128)}, f32[22,38,3]{2,1,0:T(8,128)}, u32[]{:S(2)}, u32[]{:S(2)}) collective-permute-start(f32[22,38,3]{2,1,0:T(8,128)} %get-tuple-element.59), channel_id=1, source_target_pairs={{0,1},{1,2},{2,3},{4,5},{5,6},{6,7},{8,9},{9,10},{10,11},{12,13},{... | collective-permute-start | bytes 30104 | tf_op jit(solution)/shard_map/ppermute | solution.py:32
  42.5 1.3 collective-permute-start.11
  43.8 1.4 copy.98
  45.2 1.4 copy.99
  46.6 2.5 pad_maximum_fusion
  49.3 2.3 collective-permute-done.10
  51.6 4.9 %collective-permute-done.11 = f32[22,38,3]{2,1,0:T(8,128)} collective-permute-done((f32[22,38,3]{2,1,0:T(8,128)}, f32[22,38,3]{2,1,0:T(8,128)}, u32[]{:S(2)}, u32[]{:S(2)}) %collective-permute-start.11) | collective-permute-done | bytes 10064 | tf_op jit(solution)/shard_map/ppermute | solution.py:34
  56.4 3.9 %multiply_multiply_fusion.2 = (f32[22,38,134]{2,1,0:T(8,128)S(1)}, f32[22,38,134]{2,1,0:T(8,128)S(1)}, f32[22,38,134]{2,1,0:T(8,128)S(1)}, f32[22,38,134]{2,1,0:...) fusion(f32[22,38,3]{2,1,0:T(8,128)} %collective-permute-done.11, ...), kind=kLoop, calls=%fused_computation.30 | loop fusion | flops 5377152 | bytes 8513824 | tf_op jit(solution)/shard_map/mul | solution.py:98
  60.4 3.3 %slice_add_fusion.3 = (f32[20,36,132]{2,1,0:T(8,128)S(1)}, f32[20,36,132]{2,1,0:T(8,128)S(1)}) fusion(f32[22,38,134]{2,1,0:T(8,128)S(1)} %get-tuple-element.37, f32[22,38,134]{2,1,0:T(8,128)S(1)} %get-tuple-element.46, f32[22,38,134]{2,1,0:T(8,128)S(1)} %get-tuple-element.45, f32[22,38,134]{2,1,0:T(8,128)S(1)} %get-tuple-element.44, ...), kind=kLoop, calls=%fused_computation.81 | loop fusion | flops 1805760 | bytes 6842880 | tf_op jit(solution)/shard_map/add | solution.py:102
  63.7 3.2 %fusion.69 = f32[18,34,130]{2,1,0:T(8,128)S(1)} fusion(f32[20,36,132]{2,1,0:T(8,128)S(1)} %get-tuple-element.35, f32[22,38,134]{2,1,0:T(8,128)S(1)} %get-tuple-element.38, f32[20,36,132]{2,1,0:T(8,128)S(1)} %get-tuple-element.36, f32[22,38,134]{2,1,0:T(8,128)S(1)} %get-tuple-element.46, f32[22,38,134]{2,1,0:T(8,128)S(1)} %get-tuple-element.45, ...), kind=kLoop, calls=%fused_computation.124 | loop fusion | flops 1511640 | bytes 5728320 | tf_op jit(solution)/shard_map/add | solution.py:105
  67.0 1.6 multiply_reduce_fusion.4
  68.5 4.5 %collective-permute-start.12 = (f32[3,32,128]{2,1,0:T(8,128)S(1)}, f32[3,32,128]{2,1,0:T(8,128)S(1)}, u32[]{:S(2)}, u32[]{:S(2)}) collective-permute-start(f32[3,32,128]{2,1,0:T(8,128)S(1)} %get-tuple-element.69), channel_id=1, source_target_pairs={{0,8},{8,16},{16,24},{1,9},{9,17},{17,25},{2,10},{10,18},{18,26},{... | collective-permute-start | bytes 147464 | tf_op jit(solution)/shard_map/ppermute | solution.py:32
  73.1 1.3 collective-permute-start.13
  74.4 0.4 collective-permute-done.12
  74.8 4.3 %collective-permute-done.13 = f32[3,32,128]{2,1,0:T(8,128)S(1)} collective-permute-done((f32[3,32,128]{2,1,0:T(8,128)S(1)}, f32[3,32,128]{2,1,0:T(8,128)S(1)}, u32[]{:S(2)}, u32[]{:S(2)}) %collective-permute-start.13) | collective-permute-done | bytes 49184 | tf_op jit(solution)/shard_map/ppermute | solution.py:34
  79.1 1.3 collective-permute-start.15
  80.4 3.0 %collective-permute-start.14 = (f32[22,3,128]{2,0,1:T(8,128)S(1)}, f32[22,3,128]{2,0,1:T(8,128)S(1)}, u32[]{:S(2)}, u32[]{:S(2)}) collective-permute-start(f32[22,3,128]{2,0,1:T(8,128)S(1)} %copy.104), channel_id=1, source_target_pairs={{0,4},{1,5},{2,6},{3,7},{8,12},{9,13},{10,14},{11,15},{16,20},{17,... | collective-permute-start | bytes 101384 | tf_op jit(solution)/shard_map/ppermute | solution.py:32
  83.5 0.8 collective-permute-done.14
  84.4 1.0 fusion.111
  85.4 3.5 %collective-permute-start.16 = (f32[22,38,3]{2,1,0:T(8,128)}, f32[22,38,3]{2,1,0:T(8,128)}, u32[]{:S(2)}, u32[]{:S(2)}) collective-permute-start(f32[22,38,3]{2,1,0:T(8,128)} %get-tuple-element.57), channel_id=1, source_target_pairs={{0,1},{1,2},{2,3},{4,5},{5,6},{6,7},{8,9},{9,10},{10,11},{12,13},{... | collective-permute-start | bytes 30104 | tf_op jit(solution)/shard_map/ppermute | solution.py:32
  88.9 1.3 collective-permute-start.17
  90.2 41.3 %all-reduce.2 = (f32[]{:T(128)}, f32[]{:T(128)}) all-reduce(f32[]{:T(128)} %get-tuple-element.9, f32[]{:T(128)} %get-tuple-element.8), channel_id=1, replica_groups=mesh['gx'=4,'gy'=2,'gz'=4] {'gx','gy','gz'}, use_global_device_ids=true, to_apply=%region_1.2 | all-reduce | flops 2 | bytes 16 | tf_op jit(solution)/shard_map/psum | solution.py:118
  132.7 1.8 multiply_multiply_fusion.1
  134.6 0.3 copy-done.10
  134.9 4.5 %slice_add_fusion.2 = (f32[20,36,132]{2,1,0:T(8,128)S(1)}, f32[20,36,132]{2,1,0:T(8,128)S(1)}) fusion(f32[22,38,134]{2,1,0:T(8,128)S(1)} %get-tuple-element.33, f32[22,38,134]{2,1,0:T(8,128)} %copy-done.12, f32[22,38,134]{2,1,0:T(8,128)S(1)} %copy-done.10, f32[22,38,134]{2,1,0:T(8,128)S(1)} %copy-done.7, f32[22,38,134]{2,1,0:T(8,128)S(1)} %copy-done.4, ...), kind=kLoop, calls=%fused_computation.80 | loop fusion | flops 1805760 | bytes 6842880 | tf_op jit(solution)/shard_map/add | solution.py:102
  139.4 3.2 %fusion.58 = f32[18,34,130]{2,1,0:T(8,128)S(1)} fusion(f32[20,36,132]{2,1,0:T(8,128)S(1)} %get-tuple-element.31, f32[22,38,134]{2,1,0:T(8,128)S(1)} %get-tuple-element.34, f32[20,36,132]{2,1,0:T(8,128)S(1)} %get-tuple-element.32, f32[22,38,134]{2,1,0:T(8,128)S(1)} %copy-done.13, f32[22,38,134]{2,1,0:T(8,128)S(1)} %copy-done.10, ...), kind=kLoop, calls=%fused_computation.106 | loop fusion | flops 1511640 | bytes 5728320 | tf_op jit(solution)/shard_map/add | solution.py:105
  142.7 3.9 %multiply_reduce_fusion.2 = (f32[]{:T(128)}, f32[]{:T(128)}, f32[16,32,128]{2,1,0:T(8,128)}, f32[16,32,128]{2,1,0:T(8,128)S(1)}, f32[16,32,128]{2,1,0:T(8,128)}, /*index=5*/f32[16,32,128]{2,1,0:T(8,128)}) fusion(f32[16,32,128]{2,1,0:T(8,128)S(1)} %copy-done.19, f32[16,32,128]{2,1,0:T(8,128)S(1)} %get-tuple-element.30, f32[]{:T(128)S(6)} %div.49, ...), kind=kLoop, calls=%fused_computation.185 | loop fusion | flops 1507326 | bytes 5505036 | tf_op jit(solution)/shard_map/reduce_sum | solution.py:119
  146.6 4.2 %collective-permute-start.18 = (f32[3,32,128]{2,1,0:T(8,128)S(1)}, f32[3,32,128]{2,1,0:T(8,128)S(1)}, u32[]{:S(2)}, u32[]{:S(2)}) collective-permute-start(f32[3,32,128]{2,1,0:T(8,128)S(1)} %get-tuple-element.67), channel_id=1, source_target_pairs={{0,8},{8,16},{16,24},{1,9},{9,17},{17,25},{2,10},{10,18},{18,26},{... | collective-permute-start | bytes 147464 | tf_op jit(solution)/shard_map/ppermute | solution.py:32
  150.8 1.3 collective-permute-start.19
  152.1 0.4 collective-permute-done.18
  152.5 4.3 %collective-permute-done.19 = f32[3,32,128]{2,1,0:T(8,128)S(1)} collective-permute-done((f32[3,32,128]{2,1,0:T(8,128)S(1)}, f32[3,32,128]{2,1,0:T(8,128)S(1)}, u32[]{:S(2)}, u32[]{:S(2)}) %collective-permute-start.19) | collective-permute-done | bytes 49184 | tf_op jit(solution)/shard_map/ppermute | solution.py:34
  156.8 1.3 collective-permute-start.21
  158.1 3.0 %collective-permute-start.20 = (f32[22,3,128]{2,0,1:T(8,128)S(1)}, f32[22,3,128]{2,0,1:T(8,128)S(1)}, u32[]{:S(2)}, u32[]{:S(2)}) collective-permute-start(f32[22,3,128]{2,0,1:T(8,128)S(1)} %copy.108), channel_id=1, source_target_pairs={{0,4},{1,5},{2,6},{3,7},{8,12},{9,13},{10,14},{11,15},{16,20},{17,... | collective-permute-start | bytes 101384 | tf_op jit(solution)/shard_map/ppermute | solution.py:32
  161.2 0.8 collective-permute-done.20
  162.1 1.0 fusion.110
  163.1 2.6 collective-permute-start.22
  165.8 1.3 collective-permute-start.23
  167.0 41.5 %all-reduce.1 = (f32[]{:T(128)}, f32[]{:T(128)}) all-reduce(f32[]{:T(128)} %get-tuple-element.13, f32[]{:T(128)} %get-tuple-element.12), channel_id=1, replica_groups=mesh['gx'=4,'gy'=2,'gz'=4] {'gx','gy','gz'}, use_global_device_ids=true, to_apply=%region_5.6 | all-reduce | flops 2 | bytes 16 | tf_op jit(solution)/shard_map/psum | solution.py:118
  212.8 1.8 multiply_multiply_fusion
  215.0 4.5 %slice_add_fusion.1 = (f32[20,36,132]{2,1,0:T(8,128)S(1)}, f32[20,36,132]{2,1,0:T(8,128)S(1)}) fusion(f32[22,38,134]{2,1,0:T(8,128)S(1)} %get-tuple-element.28, f32[22,38,134]{2,1,0:T(8,128)} %copy-done.12, f32[22,38,134]{2,1,0:T(8,128)S(1)} %copy-done.11, f32[22,38,134]{2,1,0:T(8,128)S(1)} %copy-done.8, f32[22,38,134]{2,1,0:T(8,128)S(1)} %copy-done.5, ...), kind=kLoop, calls=%fused_computation.79 | loop fusion | flops 1805760 | bytes 6842880 | tf_op jit(solution)/shard_map/add | solution.py:102
  219.6 3.2 %fusion.47 = f32[18,34,130]{2,1,0:T(8,128)S(1)} fusion(f32[20,36,132]{2,1,0:T(8,128)S(1)} %get-tuple-element.26, f32[22,38,134]{2,1,0:T(8,128)S(1)} %get-tuple-element.29, f32[20,36,132]{2,1,0:T(8,128)S(1)} %get-tuple-element.27, f32[22,38,134]{2,1,0:T(8,128)S(1)} %copy-done.14, f32[22,38,134]{2,1,0:T(8,128)S(1)} %copy-done.11, ...), kind=kLoop, calls=%fused_computation.88 | loop fusion | flops 1511640 | bytes 5728320 | tf_op jit(solution)/shard_map/add | solution.py:105
  222.8 2.8 %multiply_reduce_fusion = (f32[]{:T(128)}, f32[]{:T(128)}, f32[16,32,128]{2,1,0:T(8,128)S(1)}, f32[16,32,128]{2,1,0:T(8,128)S(1)}) fusion(f32[16,32,128]{2,1,0:T(8,128)S(1)} %copy-done.20, f32[16,32,128]{2,1,0:T(8,128)S(1)} %get-tuple-element.23, f32[16,32,128]{2,1,0:T(8,128)S(1)} %get-tuple-element.30, f32[]{:T(128)S(6)} %div.50, f32[]{:T(128)S(6)} %div.52, ...), kind=kLoop, calls=%fused_computation.180 | loop fusion | flops 1900542 | bytes 5767184 | tf_op jit(solution)/shard_map/reduce_sum | solution.py:119
  225.6 41.7 %all-reduce = (f32[]{:T(128)}, f32[]{:T(128)}) all-reduce(f32[]{:T(128)} %get-tuple-element.11, f32[]{:T(128)} %get-tuple-element.10), channel_id=1, replica_groups=mesh['gx'=4,'gy'=2,'gz'=4] {'gx','gy','gz'}, use_global_device_ids=true, to_apply=%region_9.10 | all-reduce | flops 2 | bytes 16 | tf_op jit(solution)/shard_map/psum | solution.py:118
  271.3 2.0 multiply_subtract_fusion
  (105 shorter events, 1.4 us)
Async XLA Ops:
  0.6 21.1 %copy-start.17 = (f32[16,32,128]{2,1,0:T(8,128)S(1)}, f32[16,32,128]{2,1,0:T(8,128)}, u32[]{:S(2)}) copy-start(f32[16,32,128]{2,1,0:T(8,128)} %param.4) | copy-start | bytes 786436
  0.6 21.1 %copy-start.18 = (f32[16,32,128]{2,1,0:T(8,128)S(1)}, f32[16,32,128]{2,1,0:T(8,128)}, u32[]{:S(2)}) copy-start(f32[16,32,128]{2,1,0:T(8,128)} %param.3) | copy-start | bytes 786436
  1.5 14.9 %collective-permute-start.7 = (f32[3,32,128]{2,1,0:T(8,128)S(1)}, f32[3,32,128]{2,1,0:T(8,128)S(1)}, u32[]{:S(2)}, u32[]{:S(2)}) collective-permute-start(f32[3,32,128]{2,1,0:T(8,128)S(1)} %get-tuple-element.71), channel_id=1, source_target_pairs={{8,0},{16,8},{24,16},{9,1},{17,9},{25,17},{10,2},{18,10},{26,18},{... | collective-permute-start | bytes 147464 | tf_op jit(solution)/shard_map/ppermute | solution.py:34
  2.8 12.6 %collective-permute-start.6 = (f32[3,32,128]{2,1,0:T(8,128)S(1)}, f32[3,32,128]{2,1,0:T(8,128)S(1)}, u32[]{:S(2)}, u32[]{:S(2)}) collective-permute-start(f32[3,32,128]{2,1,0:T(8,128)S(1)} %get-tuple-element.72), channel_id=1, source_target_pairs={{0,8},{8,16},{16,24},{1,9},{9,17},{17,25},{2,10},{10,18},{18,26},{... | collective-permute-start | bytes 147464 | tf_op jit(solution)/shard_map/ppermute | solution.py:32
  9.3 12.4 %collective-permute-start = (f32[2,4,32,128]{3,2,1,0:T(8,128)S(1)}, f32[2,4,32,128]{3,2,1,0:T(8,128)S(1)}, u32[]{:S(2)}, u32[]{:S(2)}) collective-permute-start(f32[2,4,32,128]{3,2,1,0:T(8,128)S(1)} %get-tuple-element.53), channel_id=1, source_target_pairs={{0,8},{8,16},{16,24},{1,9},{9,17},{17,25},{2,10},{10,18},{18,26},{... | collective-permute-start | bytes 393224 | tf_op jit(solution)/shard_map/ppermute | solution.py:32
  14.1 7.6 %collective-permute-start.1 = (f32[2,4,32,128]{3,2,1,0:T(8,128)S(1)}, f32[2,4,32,128]{3,2,1,0:T(8,128)S(1)}, u32[]{:S(2)}, u32[]{:S(2)}) collective-permute-start(f32[2,4,32,128]{3,2,1,0:T(8,128)S(1)} %get-tuple-element.54), channel_id=1, source_target_pairs={{8,0},{16,8},{24,16},{9,1},{17,9},{25,17},{10,2},{18,10},{26,18},{... | collective-permute-start | bytes 393224 | tf_op jit(solution)/shard_map/ppermute | solution.py:34
  16.5 4.4 %collective-permute-start.9 = (f32[22,3,128]{2,0,1:T(8,128)S(1)}, f32[22,3,128]{2,0,1:T(8,128)S(1)}, u32[]{:S(2)}, u32[]{:S(2)}) collective-permute-start(f32[22,3,128]{2,0,1:T(8,128)S(1)} %copy.115), channel_id=1, source_target_pairs={{4,0},{5,1},{6,2},{7,3},{12,8},{13,9},{14,10},{15,11},{20,16},{21,... | collective-permute-start | bytes 101384 | tf_op jit(solution)/shard_map/ppermute | solution.py:34
  17.8 3.9 %collective-permute-start.8 = (f32[22,3,128]{2,0,1:T(8,128)S(1)}, f32[22,3,128]{2,0,1:T(8,128)S(1)}, u32[]{:S(2)}, u32[]{:S(2)}) collective-permute-start(f32[22,3,128]{2,0,1:T(8,128)S(1)} %copy.114), channel_id=1, source_target_pairs={{0,4},{1,5},{2,6},{3,7},{8,12},{9,13},{10,14},{11,15},{16,20},{17,... | collective-permute-start | bytes 101384 | tf_op jit(solution)/shard_map/ppermute | solution.py:32
  20.8 5.4 %copy-start.28 = (f32[22,3,128]{2,1,0:T(4,128)}, f32[22,3,128]{2,1,0:T(4,128)S(1)}, u32[]{:S(2)}) copy-start(f32[22,3,128]{2,1,0:T(4,128)S(1)} %copy.103) | copy-start | bytes 101380
  21.7 4.6 %copy-start.30 = (f32[22,3,128]{2,1,0:T(4,128)}, f32[22,3,128]{2,1,0:T(4,128)S(1)}, u32[]{:S(2)}) copy-start(f32[22,3,128]{2,1,0:T(4,128)S(1)} %copy.102) | copy-start | bytes 101380
  21.7 5.4 %copy-start.23 = (f32[2,4,32,128]{3,2,1,0:T(8,128)}, f32[2,4,32,128]{3,2,1,0:T(8,128)S(1)}, u32[]{:S(2)}) copy-start(f32[2,4,32,128]{3,2,1,0:T(8,128)S(1)} %collective-permute-done.1) | copy-start | bytes 393220
  21.8 4.4 %collective-permute-start.3 = (f32[2,24,4,128]{3,1,2,0:T(8,128)S(1)}, f32[2,24,4,128]{3,1,2,0:T(8,128)S(1)}, u32[]{:S(2)}, u32[]{:S(2)}) collective-permute-start(f32[2,24,4,128]{3,1,2,0:T(8,128)S(1)} %copy.113), channel_id=1, source_target_pairs={{4,0},{5,1},{6,2},{7,3},{12,8},{13,9},{14,10},{15,11},{20,16},{21,... | collective-permute-start | bytes 294920 | tf_op jit(solution)/shard_map/ppermute | solution.py:34
  23.1 4.0 %collective-permute-start.2 = (f32[2,24,4,128]{3,1,2,0:T(8,128)S(1)}, f32[2,24,4,128]{3,1,2,0:T(8,128)S(1)}, u32[]{:S(2)}, u32[]{:S(2)}) collective-permute-start(f32[2,24,4,128]{3,1,2,0:T(8,128)S(1)} %copy.112), channel_id=1, source_target_pairs={{0,4},{1,5},{2,6},{3,7},{8,12},{9,13},{10,14},{11,15},{16,20},{17,... | collective-permute-start | bytes 294920 | tf_op jit(solution)/shard_map/ppermute | solution.py:32
  27.1 0.6 copy-start.26
  31.2 15.4 %copy-start.24 = (f32[2,4,32,128]{3,2,1,0:T(8,128)S(1)}, f32[2,4,32,128]{3,2,1,0:T(8,128)}, u32[]{:S(2)}) copy-start(f32[2,4,32,128]{3,2,1,0:T(8,128)} %copy-done.23) | copy-start | bytes 393220
  31.2 15.4 %copy-start.27 = (f32[2,24,4,128]{3,2,1,0:T(4,128)S(1)}, f32[2,24,4,128]{3,2,1,0:T(4,128)}, u32[]{:S(2)}) copy-start(f32[2,24,4,128]{3,2,1,0:T(4,128)} %copy-done.26) | copy-start | bytes 294916
  31.2 14.0 %collective-permute-start.5 = (f32[2,24,40,4]{2,1,3,0:T(8,128)S(1)}, f32[2,24,40,4]{2,1,3,0:T(8,128)S(1)}, u32[]{:S(2)}, u32[]{:S(2)}) collective-permute-start(f32[2,24,40,4]{2,1,3,0:T(8,128)S(1)} %copy.97), channel_id=1, source_target_pairs={{1,0},{2,1},{3,2},{5,4},{6,5},{7,6},{9,8},{10,9},{11,10},{13,12},{... | collective-permute-start | bytes 92168 | tf_op jit(solution)/shard_map/ppermute | solution.py:34
  32.6 11.1 %collective-permute-start.4 = (f32[2,24,40,4]{2,1,3,0:T(8,128)S(1)}, f32[2,24,40,4]{2,1,3,0:T(8,128)S(1)}, u32[]{:S(2)}, u32[]{:S(2)}) collective-permute-start(f32[2,24,40,4]{2,1,3,0:T(8,128)S(1)} %copy.96), channel_id=1, source_target_pairs={{0,1},{1,2},{2,3},{4,5},{5,6},{6,7},{8,9},{9,10},{10,11},{12,13},{... | collective-permute-start | bytes 92168 | tf_op jit(solution)/shard_map/ppermute | solution.py:32
  38.2 13.3 %collective-permute-start.10 = (f32[22,38,3]{2,1,0:T(8,128)}, f32[22,38,3]{2,1,0:T(8,128)}, u32[]{:S(2)}, u32[]{:S(2)}) collective-permute-start(f32[22,38,3]{2,1,0:T(8,128)} %get-tuple-element.59), channel_id=1, source_target_pairs={{0,1},{1,2},{2,3},{4,5},{5,6},{6,7},{8,9},{9,10},{10,11},{12,13},{... | collective-permute-start | bytes 30104 | tf_op jit(solution)/shard_map/ppermute | solution.py:32
  42.5 14.0 %collective-permute-start.11 = (f32[22,38,3]{2,1,0:T(8,128)}, f32[22,38,3]{2,1,0:T(8,128)}, u32[]{:S(2)}, u32[]{:S(2)}) collective-permute-start(f32[22,38,3]{2,1,0:T(8,128)} %get-tuple-element.60), channel_id=1, source_target_pairs={{1,0},{2,1},{3,2},{5,4},{6,5},{7,6},{9,8},{10,9},{11,10},{13,12},{... | collective-permute-start | bytes 30104 | tf_op jit(solution)/shard_map/ppermute | solution.py:34
  49.1 7.3 %copy-start.29 = (f32[22,3,128]{2,1,0:T(4,128)S(1)}, f32[22,3,128]{2,1,0:T(4,128)}, u32[]{:S(2)}) copy-start(f32[22,3,128]{2,1,0:T(4,128)} %copy-done.28) | copy-start | bytes 101380
  49.1 7.3 %copy-start.31 = (f32[22,3,128]{2,1,0:T(4,128)S(1)}, f32[22,3,128]{2,1,0:T(4,128)}, u32[]{:S(2)}) copy-start(f32[22,3,128]{2,1,0:T(4,128)} %copy-done.30) | copy-start | bytes 101380
  60.3 6.6 %copy-start = (f32[22,38,134]{2,1,0:T(8,128)}, f32[22,38,134]{2,1,0:T(8,128)S(1)}, u32[]{:S(2)}) copy-start(f32[22,38,134]{2,1,0:T(8,128)S(1)} %get-tuple-element.42) | copy-start | bytes 1344292
  60.3 6.6 %copy-start.3 = (f32[22,38,134]{2,1,0:T(8,128)}, f32[22,38,134]{2,1,0:T(8,128)S(1)}, u32[]{:S(2)}) copy-start(f32[22,38,134]{2,1,0:T(8,128)S(1)} %get-tuple-element.43) | copy-start | bytes 1344292
  60.3 6.6 %copy-start.6 = (f32[22,38,134]{2,1,0:T(8,128)}, f32[22,38,134]{2,1,0:T(8,128)S(1)}, u32[]{:S(2)}) copy-start(f32[22,38,134]{2,1,0:T(8,128)S(1)} %get-tuple-element.44) | copy-start | bytes 1344292
  60.3 6.6 %copy-start.9 = (f32[22,38,134]{2,1,0:T(8,128)}, f32[22,38,134]{2,1,0:T(8,128)S(1)}, u32[]{:S(2)}) copy-start(f32[22,38,134]{2,1,0:T(8,128)S(1)} %get-tuple-element.45) | copy-start | bytes 1344292
  60.3 6.6 %copy-start.12 = (f32[22,38,134]{2,1,0:T(8,128)}, f32[22,38,134]{2,1,0:T(8,128)S(1)}, u32[]{:S(2)}) copy-start(f32[22,38,134]{2,1,0:T(8,128)S(1)} %get-tuple-element.46) | copy-start | bytes 1344292
  63.7 3.3 %copy-start.19 = (f32[16,32,128]{2,1,0:T(8,128)S(1)}, f32[16,32,128]{2,1,0:T(8,128)}, u32[]{:S(2)}) copy-start(f32[16,32,128]{2,1,0:T(8,128)} %param.5) | copy-start | bytes 786436
  66.9 1.6 copy-start.15
  68.5 6.3 %collective-permute-start.12 = (f32[3,32,128]{2,1,0:T(8,128)S(1)}, f32[3,32,128]{2,1,0:T(8,128)S(1)}, u32[]{:S(2)}, u32[]{:S(2)}) collective-permute-start(f32[3,32,128]{2,1,0:T(8,128)S(1)} %get-tuple-element.69), channel_id=1, source_target_pairs={{0,8},{8,16},{16,24},{1,9},{9,17},{17,25},{2,10},{10,18},{18,26},{... | collective-permute-start | bytes 147464 | tf_op jit(solution)/shard_map/ppermute | solution.py:32
  73.1 6.0 %collective-permute-start.13 = (f32[3,32,128]{2,1,0:T(8,128)S(1)}, f32[3,32,128]{2,1,0:T(8,128)S(1)}, u32[]{:S(2)}, u32[]{:S(2)}) collective-permute-start(f32[3,32,128]{2,1,0:T(8,128)S(1)} %get-tuple-element.70), channel_id=1, source_target_pairs={{8,0},{16,8},{24,16},{9,1},{17,9},{25,17},{10,2},{18,10},{26,18},{... | collective-permute-start | bytes 147464 | tf_op jit(solution)/shard_map/ppermute | solution.py:34
  79.1 4.4 %collective-permute-start.15 = (f32[22,3,128]{2,0,1:T(8,128)S(1)}, f32[22,3,128]{2,0,1:T(8,128)S(1)}, u32[]{:S(2)}, u32[]{:S(2)}) collective-permute-start(f32[22,3,128]{2,0,1:T(8,128)S(1)} %copy.105), channel_id=1, source_target_pairs={{4,0},{5,1},{6,2},{7,3},{12,8},{13,9},{14,10},{15,11},{20,16},{21,... | collective-permute-start | bytes 101384 | tf_op jit(solution)/shard_map/ppermute | solution.py:34
  80.4 3.9 %collective-permute-start.14 = (f32[22,3,128]{2,0,1:T(8,128)S(1)}, f32[22,3,128]{2,0,1:T(8,128)S(1)}, u32[]{:S(2)}, u32[]{:S(2)}) collective-permute-start(f32[22,3,128]{2,0,1:T(8,128)S(1)} %copy.104), channel_id=1, source_target_pairs={{0,4},{1,5},{2,6},{3,7},{8,12},{9,13},{10,14},{11,15},{16,20},{17,... | collective-permute-start | bytes 101384 | tf_op jit(solution)/shard_map/ppermute | solution.py:32
  85.4 47.2 %collective-permute-start.16 = (f32[22,38,3]{2,1,0:T(8,128)}, f32[22,38,3]{2,1,0:T(8,128)}, u32[]{:S(2)}, u32[]{:S(2)}) collective-permute-start(f32[22,38,3]{2,1,0:T(8,128)} %get-tuple-element.57), channel_id=1, source_target_pairs={{0,1},{1,2},{2,3},{4,5},{5,6},{6,7},{8,9},{9,10},{10,11},{12,13},{... | collective-permute-start | bytes 30104 | tf_op jit(solution)/shard_map/ppermute | solution.py:32
  88.9 43.8 %collective-permute-start.17 = (f32[22,38,3]{2,1,0:T(8,128)}, f32[22,38,3]{2,1,0:T(8,128)}, u32[]{:S(2)}, u32[]{:S(2)}) collective-permute-start(f32[22,38,3]{2,1,0:T(8,128)} %get-tuple-element.58), channel_id=1, source_target_pairs={{1,0},{2,1},{3,2},{5,4},{6,5},{7,6},{9,8},{10,9},{11,10},{13,12},{... | collective-permute-start | bytes 30104 | tf_op jit(solution)/shard_map/ppermute | solution.py:34
  132.6 1.9 copy-start.1
  132.6 1.9 copy-start.4
  132.6 2.0 copy-start.7
  132.6 2.2 copy-start.10
  134.9 4.5 %copy-start.13 = (f32[22,38,134]{2,1,0:T(8,128)S(1)}, f32[22,38,134]{2,1,0:T(8,128)}, u32[]{:S(2)}) copy-start(f32[22,38,134]{2,1,0:T(8,128)} %copy-done.12) | copy-start | bytes 1344292
  142.6 3.9 %copy-start.16 = (f32[18,34,130]{2,1,0:T(8,128)}, f32[18,34,130]{2,1,0:T(8,128)S(1)}, u32[]{:S(2)}) copy-start(f32[18,34,130]{2,1,0:T(8,128)S(1)} %fusion.58) | copy-start | bytes 954724
  146.6 5.9 %collective-permute-start.18 = (f32[3,32,128]{2,1,0:T(8,128)S(1)}, f32[3,32,128]{2,1,0:T(8,128)S(1)}, u32[]{:S(2)}, u32[]{:S(2)}) collective-permute-start(f32[3,32,128]{2,1,0:T(8,128)S(1)} %get-tuple-element.67), channel_id=1, source_target_pairs={{0,8},{8,16},{16,24},{1,9},{9,17},{17,25},{2,10},{10,18},{18,26},{... | collective-permute-start | bytes 147464 | tf_op jit(solution)/shard_map/ppermute | solution.py:32
  150.8 6.0 %collective-permute-start.19 = (f32[3,32,128]{2,1,0:T(8,128)S(1)}, f32[3,32,128]{2,1,0:T(8,128)S(1)}, u32[]{:S(2)}, u32[]{:S(2)}) collective-permute-start(f32[3,32,128]{2,1,0:T(8,128)S(1)} %get-tuple-element.68), channel_id=1, source_target_pairs={{8,0},{16,8},{24,16},{9,1},{17,9},{25,17},{10,2},{18,10},{26,18},{... | collective-permute-start | bytes 147464 | tf_op jit(solution)/shard_map/ppermute | solution.py:34
  156.8 4.4 %collective-permute-start.21 = (f32[22,3,128]{2,0,1:T(8,128)S(1)}, f32[22,3,128]{2,0,1:T(8,128)S(1)}, u32[]{:S(2)}, u32[]{:S(2)}) collective-permute-start(f32[22,3,128]{2,0,1:T(8,128)S(1)} %copy.109), channel_id=1, source_target_pairs={{4,0},{5,1},{6,2},{7,3},{12,8},{13,9},{14,10},{15,11},{20,16},{21,... | collective-permute-start | bytes 101384 | tf_op jit(solution)/shard_map/ppermute | solution.py:34
  158.1 3.9 %collective-permute-start.20 = (f32[22,3,128]{2,0,1:T(8,128)S(1)}, f32[22,3,128]{2,0,1:T(8,128)S(1)}, u32[]{:S(2)}, u32[]{:S(2)}) collective-permute-start(f32[22,3,128]{2,0,1:T(8,128)S(1)} %copy.108), channel_id=1, source_target_pairs={{0,4},{1,5},{2,6},{3,7},{8,12},{9,13},{10,14},{11,15},{16,20},{17,... | collective-permute-start | bytes 101384 | tf_op jit(solution)/shard_map/ppermute | solution.py:32
  163.1 49.6 %collective-permute-start.22 = (f32[22,38,3]{2,1,0:T(8,128)}, f32[22,38,3]{2,1,0:T(8,128)}, u32[]{:S(2)}, u32[]{:S(2)}) collective-permute-start(f32[22,38,3]{2,1,0:T(8,128)} %get-tuple-element.55), channel_id=1, source_target_pairs={{0,1},{1,2},{2,3},{4,5},{5,6},{6,7},{8,9},{9,10},{10,11},{12,13},{... | collective-permute-start | bytes 30104 | tf_op jit(solution)/shard_map/ppermute | solution.py:32
  165.8 47.0 %collective-permute-start.23 = (f32[22,38,3]{2,1,0:T(8,128)}, f32[22,38,3]{2,1,0:T(8,128)}, u32[]{:S(2)}, u32[]{:S(2)}) collective-permute-start(f32[22,38,3]{2,1,0:T(8,128)} %get-tuple-element.56), channel_id=1, source_target_pairs={{1,0},{2,1},{3,2},{5,4},{6,5},{7,6},{9,8},{10,9},{11,10},{13,12},{... | collective-permute-start | bytes 30104 | tf_op jit(solution)/shard_map/ppermute | solution.py:34
  212.7 1.9 copy-start.2
  212.7 1.9 copy-start.5
  212.7 2.0 copy-start.8
  212.7 2.2 copy-start.11
  215.0 4.5 %copy-start.14 = (f32[22,38,134]{2,1,0:T(8,128)S(1)}, f32[22,38,134]{2,1,0:T(8,128)}, u32[]{:S(2)}) copy-start(f32[22,38,134]{2,1,0:T(8,128)} %copy-done.12) | copy-start | bytes 1344292
  219.5 3.2 %copy-start.20 = (f32[16,32,128]{2,1,0:T(8,128)S(1)}, f32[16,32,128]{2,1,0:T(8,128)}, u32[]{:S(2)}) copy-start(f32[16,32,128]{2,1,0:T(8,128)} %get-tuple-element.22) | copy-start | bytes 786436
  219.5 3.2 %copy-start.21 = (f32[16,32,128]{2,1,0:T(8,128)S(1)}, f32[16,32,128]{2,1,0:T(8,128)}, u32[]{:S(2)}) copy-start(f32[16,32,128]{2,1,0:T(8,128)} %get-tuple-element.25) | copy-start | bytes 786436
  219.5 3.2 %copy-start.25 = (f32[16,32,128]{2,1,0:T(8,128)S(1)}, f32[16,32,128]{2,1,0:T(8,128)}, u32[]{:S(2)}) copy-start(f32[16,32,128]{2,1,0:T(8,128)} %get-tuple-element.24) | copy-start | bytes 786436
  222.8 48.5 %copy-start.22 = (f32[16,32,128]{2,1,0:T(8,128)S(1)}, f32[16,32,128]{2,1,0:T(8,128)}, u32[]{:S(2)}) copy-start(f32[16,32,128]{2,1,0:T(8,128)} %get-tuple-element.25) | copy-start | bytes 786436
where the time goes:
time: 275 us; the launch traced here: 273 us
  blocking collectives  124 us (45%)
  starting transfers between devices  61.7 us (22%)
  other arithmetic  43.7 us (16%)
  waiting for transfers between devices  19.8 us (7%)
  local copies, waits for them, and re-layouts  12.8 us (5%)
  between operations  10.8 us (4%)
    psum x3, blocking collectives, shards(): lax.psum((jnp.sum(residual * u_vec), jnp.sum(w_vec * u_vec)), ('gx', 'gy'...  124 us
    ppermute x12, starting transfers between devices, padded_2(): lax.ppermute(tail, axis, [(i, (i + 1) % count) for i in range(ends)])  46.1 us
    ppermute x12, starting transfers between devices, padded_2(): lax.ppermute(head, axis, [((i + 1) % count, i) for i in range(ends)])  15.6 us
    ppermute x12, waiting for transfers between devices, padded_2(): lax.ppermute(head, axis, [((i + 1) % count, i) for i in range(ends)])  13.4 us
    add x3, other arithmetic, apply_both(): approx = interior(approx, 1) + update  12.4 us
    add x3, other arithmetic, apply_both(): result_cycle = interior(approx, 1) + update  9.62 us
    reduce_sum x3, other arithmetic, shards(): jnp.sum(w_vec * u_vec)  8.32 us
    mul x3, other arithmetic, apply_both(): update = wide_inverse * widened * first_scale  7.49 us
  transfers between devices with their start and end apart: 24, of which 10 were waited for; matrix products, arithmetic and copies ran while one was open for 3% of the time, Pallas kernels for 0%

commit v1 on v0

v1 whole, which is shorter than its diff:
```python
import functools

import jax
import jax.numpy as jnp
from jax import lax
from jax.experimental import pallas as pl
from jax.experimental.pallas import tpu as pltpu
from jax.sharding import PartitionSpec as P

ITERS = 3
AXES = ("gx", "gy", "gz")
MESH = pl.DeviceIdType.MESH

chebyshev_low = 0.15
chebyshev_high = 2.0
chebyshev_mid = 0.5 * (chebyshev_high + chebyshev_low)
chebyshev_half = 0.5 * (chebyshev_high - chebyshev_low)
chebyshev_ratio = chebyshev_mid / chebyshev_half
rho_first = 1.0 / chebyshev_ratio
rho_second = 1.0 / (2.0 * chebyshev_ratio - rho_first)
rho_third = 1.0 / (2.0 * chebyshev_ratio - rho_second)
first_scale = 1.0 / chebyshev_mid
keep_second = rho_second * rho_first
push_second = 2.0 * rho_second / chebyshev_half
keep_third = rho_third * rho_second
push_third = 2.0 * rho_third / chebyshev_half

ROUNDS = 1 + 3 * ITERS


def harmonic(a, b):
    return 2.0 * a * b / (a + b)


def conjugate_gradients(moments):
    def product(left, right):
        total = None
        for i, a in enumerate(left):
            for j, b in enumerate(right):
                term = a * b * moments[i + j]
                total = term if total is None else total + term
        return total

    def through_operator(c):
        return [c[0]] + [c[j] - c[j - 1] for j in range(1, len(c))] + [-c[-1]]

    def axpy(x, scale, y):
        out = []
        for j in range(max(len(x), len(y))):
            if j >= len(y):
                out.append(x[j])
            elif j >= len(x):
                out.append(scale * y[j])
            else:
                out.append(x[j] + scale * y[j])
        return out

    residual = [jnp.ones_like(moments[0])]
    pressure, direction = [], []
    gamma_prev = alpha_prev = None
    for iteration in range(ITERS):
        image = through_operator(residual)
        gamma = product(residual, residual)
        curvature = product(image, residual)
        if iteration == 0:
            alpha = gamma / curvature
            direction = list(residual)
        else:
            beta = gamma / gamma_prev
            alpha = gamma / (curvature - beta * gamma / alpha_prev)
            direction = axpy(residual, beta, direction)
        pressure = axpy(pressure, alpha, direction) if pressure else [alpha * d for d in direction]
        residual = axpy(residual, -alpha, through_operator(direction))
        gamma_prev, alpha_prev = gamma, alpha
    return pressure, residual


def kernel(
    sizes,
    cond_hbm, reac_hbm, src_hbm, press_ref, resid_ref,
    cond, reac, src, diag, coef, fields, zs, dvec, hacc,
    halo_x, halo_y, halo_z, stage_y, stage_z, sums_out, sums_in,
    load_sem, send_sem, recv_sem, sum_send, sum_recv,
):
    bx, by, bz = cond.shape
    tiles = by // 8
    me = [lax.axis_index(a) for a in AXES]

    loads = [
        pltpu.make_async_copy(h, v, load_sem.at[i])
        for i, (h, v) in enumerate(((cond_hbm, cond), (reac_hbm, reac), (src_hbm, src)))
    ]
    for load in loads:
        load.start()

    halo_x[...] = jnp.zeros_like(halo_x)
    halo_y[...] = jnp.zeros_like(halo_y)
    halo_z[...] = jnp.zeros_like(halo_z)

    def peer(axis, index):
        return tuple(index if a == axis else me[a] for a in range(3))

    barrier = pltpu.get_barrier_semaphore()
    for axis in range(3):
        for off in range(1, sizes[axis]):
            pl.semaphore_signal(
                barrier, inc=1,
                device_id=peer(axis, lax.rem(me[axis] + off, sizes[axis])),
                device_id_type=MESH,
            )
    pl.semaphore_wait(barrier, sum(s - 1 for s in sizes))

    def face_copy(e, axis, up):
        side = 0 if up else 1
        lane = 2 * axis + side
        if axis == 0:
            plane = bx - 1 if up else 0
            source = fields.at[e, plane]
            target = halo_x.at[e, side]
        elif axis == 1:
            source = stage_y.at[e, side]
            target = halo_y.at[e, side]
        else:
            source = stage_z.at[e]
            target = halo_z.at[e, side]
        return pltpu.make_async_remote_copy(
            src_ref=source, dst_ref=target,
            send_sem=send_sem.at[e, lane], recv_sem=recv_sem.at[e, lane],
            device_id=peer(axis, me[axis] + (1 if up else -1)),
            device_id_type=MESH,
        )

    def exists(axis, up):
        return me[axis] < sizes[axis] - 1 if up else me[axis] > 0

    def send(e, axis):
        for up in (True, False):
            @pl.when(exists(axis, up))
            def _():
                face_copy(e, axis, up).start()

    def receive(e):
        for axis in range(3):
            for up in (True, False):
                @pl.when(exists(axis, not up))
                def _():
                    face_copy(e, axis, up).wait_recv()

    def sent(e):
        for axis in range(3):
            for up in (True, False):
                @pl.when(exists(axis, up))
                def _():
                    face_copy(e, axis, up).wait_send()

    lanes8 = lax.broadcasted_iota(jnp.int32, (8, bz), 1)
    pair8 = lanes8 // 2
    lanes = lax.broadcasted_iota(jnp.int32, (by, bz), 1)
    rows = lax.broadcasted_iota(jnp.int32, (by, bz), 0)
    order = [0, bx - 1] + list(range(1, bx - 1))

    def emit(e, x, plane, packs):
        fields[e, x] = plane
        stage_y[e, 0, pl.ds(x, 1), :] = plane[by - 1:by, :]
        stage_y[e, 1, pl.ds(x, 1), :] = plane[0:1, :]
        for t in range(tiles):
            idx = x * tiles + t
            rolled = pltpu.roll(plane[8 * t:8 * t + 8, :], (2 * idx + 1) % bz, 1)
            packs[t] = jnp.where(pair8 == idx, rolled, packs[t])

    def finish(e, packs):
        total = packs[0]
        for t in range(1, tiles):
            total = jnp.where(pair8 % tiles == t, packs[t], total)
        stage_z[e] = total
        send(e, 2)
        send(e, 1)

    def edge_lanes(e):
        from_upper = pltpu.roll(halo_z[e, 1], bz - 1, 1)
        from_lower = pltpu.roll(halo_z[e, 0], 1, 1)
        return jnp.where(lanes8 % 2 == 0, from_upper, from_lower)

    def neighbours(e, x, edges, plane):
        low_x = fields[e, x - 1] if x > 0 else halo_x[e, 0]
        up_x = fields[e, x + 1] if x < bx - 1 else halo_x[e, 1]
        low_y = jnp.where(rows == 0, halo_y[e, 0, pl.ds(x, 1), :], pltpu.roll(plane, 1, 0))
        up_y = jnp.where(rows == by - 1, halo_y[e, 1, pl.ds(x, 1), :], pltpu.roll(plane, by - 1, 0))
        edge = jnp.concatenate(
            [
                pltpu.roll(edges, (bz - (2 * (x * tiles + t) + 1)) % bz, 1)
                for t in range(tiles)
            ],
            axis=0,
        )
        low_z = jnp.where(lanes == 0, edge, pltpu.roll(plane, 1, 1))
        up_z = jnp.where(lanes == bz - 1, edge, pltpu.roll(plane, bz - 1, 1))
        return low_x, up_x, low_y, up_y, low_z, up_z

    def blank():
        return [jnp.zeros((8, bz), jnp.float32) for _ in range(tiles)]

    loads[0].wait()
    packs = blank()
    for x in order:
        emit(0, x, cond[x], packs)
        if x == bx - 1:
            send(0, 0)
    finish(0, packs)
    loads[1].wait()
    loads[2].wait()
    receive(0)
    edges = edge_lanes(0)
    packs = blank()
    for x in order:
        mine = cond[x]
        faces = [harmonic(mine, other) for other in neighbours(0, x, edges, mine)]
        total = reac[x]
        for face in faces:
            total = total + face
        inverse = 1.0 / total
        diag[x] = total
        for n, face in enumerate(faces):
            coef[n, x] = face * inverse
        first = inverse * src[x]
        zs[0, x] = first
        first = first * first_scale
        dvec[x] = first
        emit(1, x, first, packs)
        if x == bx - 1:
            send(1, 0)
    finish(1, packs)

    def residue(e, k, x, edges):
        plane = fields[e, x]
        total = zs[k, x] - plane
        for n, other in enumerate(neighbours(e, x, edges, plane)):
            total = total + coef[n, x] * other
        return plane, total

    def step(k, last):
        for s, (keep, push) in enumerate(((keep_second, push_second), (keep_third, push_third))):
            e = 3 * k + 1 + s
            receive(e)
            edges = edge_lanes(e)
            packs = blank()
            for x in order:
                plane, rest = residue(e, k, x, edges)
                update = keep * dvec[x] + push * rest
                if s == 0:
                    dvec[x] = update
                emit(e + 1, x, plane + update, packs)
                if x == bx - 1:
                    send(e + 1, 0)
            finish(e + 1, packs)
        e = 3 * k + 3
        receive(e)
        edges = edge_lanes(e)
        packs = blank()
        even = odd = None
        for x in order:
            plane, rest = residue(e, k, x, edges)
            weighted = diag[x] * plane
            a, b = weighted * zs[k, x], weighted * rest
            even = a if even is None else even + a
            odd = b if odd is None else odd + b
            zs[k + 1, x] = rest
            if not last:
                first = rest * first_scale
                dvec[x] = first
                emit(e + 1, x, first, packs)
                if x == bx - 1:
                    send(e + 1, 0)
        if not last:
            finish(e + 1, packs)
        hacc[pl.ds(2 * k, 1), :] = jnp.sum(even, axis=0, keepdims=True)
        hacc[pl.ds(2 * k + 1, 1), :] = jnp.sum(odd, axis=0, keepdims=True)

    hacc[...] = jnp.zeros_like(hacc)

    def body(k, carry):
        step(k, False)
        return carry

    lax.fori_loop(0, ITERS - 1, body, 0)
    step(ITERS - 1, True)

    total = hacc[...]
    base = 0
    for axis in range(3):
        sums_out[axis] = total
        copies = []
        for off in range(1, sizes[axis]):
            slot = base + off - 1
            copies.append(
                pltpu.make_async_remote_copy(
                    src_ref=sums_out.at[axis], dst_ref=sums_in.at[slot],
                    send_sem=sum_send.at[slot], recv_sem=sum_recv.at[slot],
                    device_id=peer(axis, lax.rem(me[axis] + off, sizes[axis])),
                    device_id_type=MESH,
                )
            )
        for copy in copies:
            copy.start()
        for n, copy in enumerate(copies):
            copy.wait_recv()
            total = total + sums_in[base + n]
        for copy in copies:
            copy.wait_send()
        base += sizes[axis] - 1

    row8 = lax.broadcasted_iota(jnp.int32, (8, bz), 0)
    moments = [
        jnp.full((8, bz), jnp.sum(jnp.where(row8 == n, total, 0.0)), jnp.float32)
        for n in range(2 * ITERS)
    ]
    pressure, residual = conjugate_gradients(moments)
    pressure = [jnp.concatenate([c] * tiles, axis=0) for c in pressure]
    residual = [jnp.concatenate([c] * tiles, axis=0) for c in residual]
    for x in range(bx):
        out = pressure[0] * fields[3, x]
        for j in range(1, ITERS):
            out = out + pressure[j] * fields[3 * j + 3, x]
        press_ref[x] = out
        out = residual[0] * zs[0, x]
        for j in range(1, ITERS + 1):
            out = out + residual[j] * zs[j, x]
        resid_ref[x] = diag[x] * out

    for e in range(ROUNDS):
        sent(e)


def solution(mesh):
    sizes = tuple(mesh.shape[a] for a in AXES)
    peers = sum(s - 1 for s in sizes)

    def shards(conductance, reaction, source):
        bx, by, bz = conductance.shape
        block = (bx, by, bz)
        f32 = jnp.float32
        return pl.pallas_call(
            functools.partial(kernel, sizes),
            out_shape=(jax.ShapeDtypeStruct(block, f32),) * 2,
            in_specs=[pl.BlockSpec(memory_space=pl.ANY)] * 3,
            out_specs=(pl.BlockSpec(memory_space=pltpu.VMEM),) * 2,
            scratch_shapes=[
                pltpu.VMEM(block, f32),
                pltpu.VMEM(block, f32),
                pltpu.VMEM(block, f32),
                pltpu.VMEM(block, f32),
                pltpu.VMEM((6,) + block, f32),
                pltpu.VMEM((ROUNDS,) + block, f32),
                pltpu.VMEM((ITERS + 1,) + block, f32),
                pltpu.VMEM(block, f32),
                pltpu.VMEM((8, bz), f32),
                pltpu.VMEM((ROUNDS, 2, by, bz), f32),
                pltpu.VMEM((ROUNDS, 2, bx, bz), f32),
                pltpu.VMEM((ROUNDS, 2, 8, bz), f32),
                pltpu.VMEM((ROUNDS, 2, bx, bz), f32),
                pltpu.VMEM((ROUNDS, 8, bz), f32),
                pltpu.VMEM((3, 8, bz), f32),
                pltpu.VMEM((peers, 8, bz), f32),
                pltpu.SemaphoreType.DMA((3,)),
                pltpu.SemaphoreType.DMA((ROUNDS, 6)),
                pltpu.SemaphoreType.DMA((ROUNDS, 6)),
                pltpu.SemaphoreType.DMA((peers,)),
                pltpu.SemaphoreType.DMA((peers,)),
            ],
            compiler_params=pltpu.CompilerParams(
                collective_id=0, has_side_effects=True,
                vmem_limit_bytes=24 * 1024 * 1024,
            ),
        )(conductance, reaction, source)

    placed = P("gx", "gy", "gz")
    return jax.shard_map(
        shards,
        mesh=mesh,
        in_specs=(placed,) * 3,
        out_specs=(placed,) * 2,
        check_vma=False,
    )
```

time: 275 us -> 53.3 us (0.19)
  blocking collectives: 124 us -> 0 us
  starting transfers between devices: 61.7 us -> 0 us
  Pallas kernels: 0 us -> 48.2 us
  other arithmetic: 43.7 us -> 0 us
  waiting for transfers between devices: 19.8 us -> 0 us
  between operations: 10.8 us -> 0.65 us
  local copies, waits for them, and re-layouts: 12.8 us -> 4.25 us
    psum x3 -> x0, blocking collectives: 124 us -> none  [shards(): lax.psum((jnp.sum(residual * u_vec), jnp.sum(w_vec * u_vec)), ('gx', 'gy'...]
    ppermute x24 -> x0, starting transfers between devices: 61.7 us -> none  [the longest x12 46.1 us: padded_2(): lax.ppermute(tail, axis, [(i, (i + 1) % count) for i in range(ends)])]
    pallas_call x0 -> x1, Pallas kernels: none -> 48.2 us  [shards(): pl.pallas_call(functools.partial(kernel, sizes), out_shape=(jax.ShapeDtyp...]
    add x6 -> x0, other arithmetic: 22 us -> none  [the longest x3 12.4 us: apply_both(): approx = interior(approx, 1) + update]
    ppermute x24 -> x0, waiting for transfers between devices: 19.8 us -> none  [the longest x12 13.4 us: padded_2(): lax.ppermute(head, axis, [((i + 1) % count, i) for i in range(ends)])]
    reduce_sum x3 -> x0, other arithmetic: 8.32 us -> none  [shards(): jnp.sum(w_vec * u_vec)]
    mul x3 -> x0, other arithmetic: 7.49 us -> none  [apply_both(): update = wide_inverse * widened * first_scale]
    slice x14 -> x0, local copies, waits for them, and re-layouts: 7.32 us -> none  [the longest x10 6.02 us: padded_2(): lax.slice_in_dim(cells, cells.shape[dim] - width, cells.shape[dim], axis=...]
  transfers between devices with their start and end apart: 24 -> 0, of which waited for: 10 -> 0; matrix products, arithmetic and copies ran while one was open for 3% -> 0% of each run, Pallas kernels for 0% -> 0%
where the time goes in v1:
time: 53.3 us; the launch traced here: 53.1 us
  Pallas kernels  48.2 us (90%)
  local copies, waits for them, and re-layouts  4.25 us (8%)
  between operations  0.65 us (1%)
    pallas_call x1, Pallas kernels, shards(): pl.pallas_call(functools.partial(kernel, sizes), out_shape=(jax.ShapeDtyp...  48.2 us
    unnamed x8, local copies, waits for them, and re-layouts  4.25 us

profile of v1, /device:TPU:0, one launch (start us, length us, event | category | flops | bytes accessed | tf_op | source)
XLA Modules:
  0.0 53.1 jit_solution(12613339946713763734)
XLA Ops:
  0.6 0.0 copy-start
  0.6 0.9 %copy-done = f32[16,32,128]{2,1,0:T(8,128)S(1)} copy-done((f32[16,32,128]{2,1,0:T(8,128)S(1)}, f32[16,32,128]{2,1,0:T(8,128)}, u32[]{:S(2)}) %copy-start) | copy-done | bytes 262168
  1.6 0.0 copy-start.1
  1.6 0.9 %copy-done.1 = f32[16,32,128]{2,1,0:T(8,128)S(1)} copy-done((f32[16,32,128]{2,1,0:T(8,128)S(1)}, f32[16,32,128]{2,1,0:T(8,128)}, u32[]{:S(2)}) %copy-start.1) | copy-done | bytes 262168
  2.5 0.0 copy-start.2
  2.5 0.9 %copy-done.2 = f32[16,32,128]{2,1,0:T(8,128)S(1)} copy-done((f32[16,32,128]{2,1,0:T(8,128)S(1)}, f32[16,32,128]{2,1,0:T(8,128)}, u32[]{:S(2)}) %copy-start.2) | copy-done | bytes 262168
  3.5 48.2 %shard_map.50 = (f32[16,32,128]{2,1,0:T(8,128)S(1)}, f32[16,32,128]{2,1,0:T(8,128)S(1)}) custom-call(f32[16,32,128]{2,1,0:T(8,128)S(1)} %copy-done, f32[16,32,128]{2,1,0:T(8,128)S(1)} %copy-done.1, f32[16,32,128]{2,1,0:T(8,128)S(1)} %copy-done.2), custom_call_target="tpu_custom_call" | custom-call | tf_op jit(solution)/shard_map/pallas_call | solution.py:342
  51.7 0.7 %copy.7 = f32[16,32,128]{2,1,0:T(8,128)} copy(f32[16,32,128]{2,1,0:T(8,128)S(1)} %get-tuple-element.4) | data formatting | bytes 524288
  52.4 0.7 %copy.8 = f32[16,32,128]{2,1,0:T(8,128)} copy(f32[16,32,128]{2,1,0:T(8,128)S(1)} %get-tuple-element.5) | data formatting | bytes 524288
Async XLA Ops:
  0.6 1.0 %copy-start = (f32[16,32,128]{2,1,0:T(8,128)S(1)}, f32[16,32,128]{2,1,0:T(8,128)}, u32[]{:S(2)}) copy-start(f32[16,32,128]{2,1,0:T(8,128)} %cond_hbm.1) | copy-start | bytes 786436
  1.6 0.9 %copy-start.1 = (f32[16,32,128]{2,1,0:T(8,128)S(1)}, f32[16,32,128]{2,1,0:T(8,128)}, u32[]{:S(2)}) copy-start(f32[16,32,128]{2,1,0:T(8,128)} %reac_hbm.1) | copy-start | bytes 786436
  2.5 0.9 %copy-start.2 = (f32[16,32,128]{2,1,0:T(8,128)S(1)}, f32[16,32,128]{2,1,0:T(8,128)}, u32[]{:S(2)}) copy-start(f32[16,32,128]{2,1,0:T(8,128)} %src_hbm.1) | copy-start | bytes 786436

commit v2 on v1

--- a/solution.py
+++ b/solution.py
@@ -26,6 +26,16 @@
 push_third = 2.0 * rho_third / chebyshev_half
 
 ROUNDS = 1 + 3 * ITERS
+
+
+def sum_phases(sizes):
+    groups = [(1,), (0, 2)] if sizes[0] * sizes[2] <= 32 else [(1,), (0,), (2,)]
+    phases = []
+    for group in groups:
+        spans = [range(sizes[a]) if a in group else range(1) for a in range(3)]
+        offsets = [(i, j, k) for i in spans[0] for j in spans[1] for k in spans[2]]
+        phases.append(offsets[1:])
+    return phases
 
 
 def harmonic(a, b):
@@ -78,7 +88,7 @@
 def kernel(
     sizes,
     cond_hbm, reac_hbm, src_hbm, press_ref, resid_ref,
-    cond, reac, src, diag, coef, fields, zs, dvec, hacc,
+    cond, reac, src, diag, coef, edge_y, edge_z, fields, zs, hacc,
     halo_x, halo_y, halo_z, stage_y, stage_z, sums_out, sums_in,
     load_sem, send_sem, recv_sem, sum_send, sum_recv,
 ):
@@ -100,15 +110,19 @@
     def peer(axis, index):
         return tuple(index if a == axis else me[a] for a in range(3))
 
+    phases = sum_phases(sizes)
+
+    def at_offset(offset):
+        return tuple(lax.rem(me[a] + offset[a], sizes[a]) if offset[a] else me[a] for a in range(3))
+
+    everyone = sorted({offset for phase in phases for offset in phase} | {
+        tuple((o % sizes[a]) if a == axis else 0 for a in range(3))
+        for axis in range(3) for o in (1, -1) if sizes[axis] > 1
+    })
     barrier = pltpu.get_barrier_semaphore()
-    for axis in range(3):
-        for off in range(1, sizes[axis]):
-            pl.semaphore_signal(
-                barrier, inc=1,
-                device_id=peer(axis, lax.rem(me[axis] + off, sizes[axis])),
-                device_id_type=MESH,
-            )
-    pl.semaphore_wait(barrier, sum(s - 1 for s in sizes))
+    for offset in everyone:
+        pl.semaphore_signal(barrier, inc=1, device_id=at_offset(offset), device_id_type=MESH)
+    pl.semaphore_wait(barrier, len(everyone))
 
     def face_copy(e, axis, up):
         side = 0 if up else 1
@@ -159,20 +173,26 @@
     rows = lax.broadcasted_iota(jnp.int32, (by, bz), 0)
     order = [0, bx - 1] + list(range(1, bx - 1))
 
+    def pack(x, plane, packs):
+        for t in range(tiles):
+            idx = x * tiles + t
+            rolled = pltpu.roll(plane[8 * t:8 * t + 8, :], (2 * idx + 1) % bz, 1)
+            packs[t] = jnp.where(pair8 == idx, rolled, packs[t])
+
+    def merge(packs):
+        total = packs[0]
+        for t in range(1, tiles):
+            total = jnp.where(pair8 % tiles == t, packs[t], total)
+        return total
+
     def emit(e, x, plane, packs):
         fields[e, x] = plane
         stage_y[e, 0, pl.ds(x, 1), :] = plane[by - 1:by, :]
         stage_y[e, 1, pl.ds(x, 1), :] = plane[0:1, :]
-        for t in range(tiles):
-            idx = x * tiles + t
-            rolled = pltpu.roll(plane[8 * t:8 * t + 8, :], (2 * idx + 1) % bz, 1)
-            packs[t] = jnp.where(pair8 == idx, rolled, packs[t])
+        pack(x, plane, packs)
 
     def finish(e, packs):
-        total = packs[0]
-        for t in range(1, tiles):
-            total = jnp.where(pair8 % tiles == t, packs[t], total)
-        stage_z[e] = total
+        stage_z[e] = merge(packs)
         send(e, 2)
         send(e, 1)
 
@@ -211,7 +231,7 @@
     loads[2].wait()
     receive(0)
     edges = edge_lanes(0)
-    packs = blank()
+    packs, edge_packs = blank(), blank()
     for x in order:
         mine = cond[x]
         faces = [harmonic(mine, other) for other in neighbours(0, x, edges, mine)]
@@ -220,61 +240,101 @@
             total = total + face
         inverse = 1.0 / total
         diag[x] = total
-        for n, face in enumerate(faces):
-            coef[n, x] = face * inverse
+        faces = [face * inverse for face in faces]
         first = inverse * src[x]
         zs[0, x] = first
-        first = first * first_scale
-        dvec[x] = first
-        emit(1, x, first, packs)
+        emit(1, x, first * first_scale, packs)
         if x == bx - 1:
             send(1, 0)
+        coef[0, x] = faces[0]
+        coef[1, x] = faces[1]
+        edge_y[0, pl.ds(x, 1), :] = faces[2][0:1, :]
+        edge_y[1, pl.ds(x, 1), :] = faces[3][by - 1:by, :]
+        coef[2, x] = jnp.where(rows == 0, 0.0, faces[2])
+        coef[3, x] = jnp.where(rows == by - 1, 0.0, faces[3])
+        coef[4, x] = jnp.where(lanes == 0, 0.0, faces[4])
+        coef[5, x] = jnp.where(lanes == bz - 1, 0.0, faces[5])
+        pack(x, jnp.where(lanes == 0, faces[4], faces[5]), edge_packs)
     finish(1, packs)
-
-    def residue(e, k, x, edges):
+    edge_z[...] = merge(edge_packs)
+
+    row8 = lax.broadcasted_iota(jnp.int32, (8, bz), 0)
+    ends8 = (lanes8 == 0) | (lanes8 == bz - 1)
+
+    def inner(e, k, x):
         plane = fields[e, x]
         total = zs[k, x] - plane
-        for n, other in enumerate(neighbours(e, x, edges, plane)):
-            total = total + coef[n, x] * other
+        if x > 0:
+            total = total + coef[0, x] * fields[e, x - 1]
+        if x < bx - 1:
+            total = total + coef[1, x] * fields[e, x + 1]
+        total = total + coef[2, x] * pltpu.roll(plane, 1, 0)
+        total = total + coef[3, x] * pltpu.roll(plane, by - 1, 0)
+        total = total + coef[4, x] * pltpu.roll(plane, 1, 1)
+        total = total + coef[5, x] * pltpu.roll(plane, bz - 1, 1)
         return plane, total
 
+    def outer(e, x, packed):
+        pieces = []
+        for t in range(tiles):
+            shift = (bz - (2 * (x * tiles + t) + 1)) % bz
+            piece = jnp.where(ends8, pltpu.roll(packed, shift, 1), 0.0)
+            if t == 0:
+                row = edge_y[0, pl.ds(x, 1), :] * halo_y[e, 0, pl.ds(x, 1), :]
+                piece = piece + jnp.where(row8 == 0, row, 0.0)
+            if t == tiles - 1:
+                row = edge_y[1, pl.ds(x, 1), :] * halo_y[e, 1, pl.ds(x, 1), :]
+                piece = piece + jnp.where(row8 == 7, row, 0.0)
+            pieces.append(piece)
+        total = jnp.concatenate(pieces, axis=0)
+        if x == 0:
+            total = total + coef[0, x] * halo_x[e, 0]
+        if x == bx - 1:
+            total = total + coef[1, x] * halo_x[e, 1]
+        return total
+
+    def moment(k, j):
+        total = None
+        for x in range(bx):
+            term = diag[x] * fields[3 * k + 3, x] * zs[j, x]
+            total = term if total is None else total + term
+        hacc[pl.ds(k + j, 1), :] = jnp.sum(total, axis=0, keepdims=True)
+
     def step(k, last):
-        for s, (keep, push) in enumerate(((keep_second, push_second), (keep_third, push_third))):
+        for s in range(2):
             e = 3 * k + 1 + s
+            push = push_third if s else push_second
+            for x in range(bx):
+                plane, rest = inner(e, k, x)
+                before = plane - fields[e - 1, x] if s else plane
+                keep = keep_third if s else keep_second
+                fields[e + 1, x] = plane + (keep * before + push * rest)
             receive(e)
-            edges = edge_lanes(e)
+            packed = edge_z[...] * edge_lanes(e)
             packs = blank()
             for x in order:
-                plane, rest = residue(e, k, x, edges)
-                update = keep * dvec[x] + push * rest
-                if s == 0:
-                    dvec[x] = update
-                emit(e + 1, x, plane + update, packs)
+                emit(e + 1, x, fields[e + 1, x] + push * outer(e, x, packed), packs)
                 if x == bx - 1:
                     send(e + 1, 0)
             finish(e + 1, packs)
         e = 3 * k + 3
+        for x in range(bx):
+            plane, rest = inner(e, k, x)
+            zs[k + 1, x] = rest
+        moment(k, k)
         receive(e)
-        edges = edge_lanes(e)
+        packed = edge_z[...] * edge_lanes(e)
         packs = blank()
-        even = odd = None
         for x in order:
-            plane, rest = residue(e, k, x, edges)
-            weighted = diag[x] * plane
-            a, b = weighted * zs[k, x], weighted * rest
-            even = a if even is None else even + a
-            odd = b if odd is None else odd + b
+            rest = zs[k + 1, x] + outer(e, x, packed)
             zs[k + 1, x] = rest
             if not last:
-                first = rest * first_scale
-                dvec[x] = first
-                emit(e + 1, x, first, packs)
+                emit(e + 1, x, rest * first_scale, packs)
                 if x == bx - 1:
                     send(e + 1, 0)
         if not last:
             finish(e + 1, packs)
-        hacc[pl.ds(2 * k, 1), :] = jnp.sum(even, axis=0, keepdims=True)
-        hacc[pl.ds(2 * k + 1, 1), :] = jnp.sum(odd, axis=0, keepdims=True)
+        moment(k, k + 1)
 
     hacc[...] = jnp.zeros_like(hacc)
 
@@ -287,29 +347,26 @@
 
     total = hacc[...]
     base = 0
-    for axis in range(3):
-        sums_out[axis] = total
+    for n, offsets in enumerate(phases):
+        sums_out[n] = total
         copies = []
-        for off in range(1, sizes[axis]):
-            slot = base + off - 1
+        for slot, offset in enumerate(offsets, base):
             copies.append(
                 pltpu.make_async_remote_copy(
-                    src_ref=sums_out.at[axis], dst_ref=sums_in.at[slot],
+                    src_ref=sums_out.at[n], dst_ref=sums_in.at[slot],
                     send_sem=sum_send.at[slot], recv_sem=sum_recv.at[slot],
-                    device_id=peer(axis, lax.rem(me[axis] + off, sizes[axis])),
-                    device_id_type=MESH,
+                    device_id=at_offset(offset), device_id_type=MESH,
                 )
             )
         for copy in copies:
             copy.start()
-        for n, copy in enumerate(copies):
+        for slot, copy in enumerate(copies, base):
             copy.wait_recv()
-            total = total + sums_in[base + n]
+            total = total + sums_in[slot]
         for copy in copies:
             copy.wait_send()
-        base += sizes[axis] - 1
-
-    row8 = lax.broadcasted_iota(jnp.int32, (8, bz), 0)
+        base += len(offsets)
+
     moments = [
         jnp.full((8, bz), jnp.sum(jnp.where(row8 == n, total, 0.0)), jnp.float32)
         for n in range(2 * ITERS)
@@ -333,7 +390,7 @@
 
 def solution(mesh):
     sizes = tuple(mesh.shape[a] for a in AXES)
-    peers = sum(s - 1 for s in sizes)
+    peers = sum(len(phase) for phase in sum_phases(sizes))
 
     def shards(conductance, reaction, source):
         bx, by, bz = conductance.shape
@@ -350,9 +407,10 @@
                 pltpu.VMEM(block, f32),
                 pltpu.VMEM(block, f32),
                 pltpu.VMEM((6,) + block, f32),
+                pltpu.VMEM((2, bx, bz), f32),
+                pltpu.VMEM((8, bz), f32),
                 pltpu.VMEM((ROUNDS,) + block, f32),
                 pltpu.VMEM((ITERS + 1,) + block, f32),
-                pltpu.VMEM(block, f32),
                 pltpu.VMEM((8, bz), f32),
                 pltpu.VMEM((ROUNDS, 2, by, bz), f32),
                 pltpu.VMEM((ROUNDS, 2, bx, bz), f32),
@@ -369,7 +427,7 @@
             ],
             compiler_params=pltpu.CompilerParams(
                 collective_id=0, has_side_effects=True,
-                vmem_limit_bytes=24 * 1024 * 1024,
+                vmem_limit_bytes=60 * 1024 * 1024,
             ),
         )(conductance, reaction, source)
 

time: 53.3 us -> 51.5 us (0.966)
  local copies, waits for them, and re-layouts: 4.25 us -> 2.42 us
    unnamed x8 -> x4, local copies, waits for them, and re-layouts: 4.25 us -> 2.42 us
where the time goes in v2:
time: 51.5 us; the launch traced here: 51.4 us
  Pallas kernels  48.3 us (94%)
  local copies, waits for them, and re-layouts  2.42 us (5%)
  between operations  0.65 us (1%)
    pallas_call x1, Pallas kernels, shards(): pl.pallas_call(functools.partial(kernel, sizes), out_shape=(jax.ShapeDtyp...  48.3 us
    unnamed x4, local copies, waits for them, and re-layouts  2.42 us

profile of v2, /device:TPU:0, one launch (start us, length us, event | category | flops | bytes accessed | tf_op | source)
XLA Modules:
  0.0 51.4 jit_solution(16562375671453216302)
XLA Ops:
  0.6 48.3 %shard_map.50 = (f32[16,32,128]{2,1,0:T(8,128)}, f32[16,32,128]{2,1,0:T(8,128)}) custom-call(f32[16,32,128]{2,1,0:T(8,128)} %cond_hbm.1, f32[16,32,128]{2,1,0:T(8,128)} %reac_hbm.1, f32[16,32,128]{2,1,0:T(8,128)} %src_hbm.1), custom_call_target="tpu_custom_call" | custom-call | tf_op jit(solution)/shard_map/pallas_call | solution.py:399
  49.0 0.0 copy-start
  49.0 1.7 %copy.7 = f32[16,32,128]{2,1,0:T(8,128)} copy(f32[16,32,128]{2,1,0:T(8,128)} %get-tuple-element.4) | data formatting | bytes 524288
  50.7 0.0 copy-done
  50.7 0.7 %copy.8 = f32[16,32,128]{2,1,0:T(8,128)} copy(f32[16,32,128]{2,1,0:T(8,128)S(1)} %copy-done) | data formatting | bytes 524288
Async XLA Ops:
  49.0 1.7 %copy-start = (f32[16,32,128]{2,1,0:T(8,128)S(1)}, f32[16,32,128]{2,1,0:T(8,128)}, u32[]{:S(2)}) copy-start(f32[16,32,128]{2,1,0:T(8,128)} %get-tuple-element.5) | copy-start | bytes 786436

commit v3 on v2

--- a/solution.py
+++ b/solution.py
@@ -399,7 +399,7 @@
         return pl.pallas_call(
             functools.partial(kernel, sizes),
             out_shape=(jax.ShapeDtypeStruct(block, f32),) * 2,
-            in_specs=[pl.BlockSpec(memory_space=pl.ANY)] * 3,
+            in_specs=[pl.BlockSpec(memory_space=pltpu.HBM)] * 3,
             out_specs=(pl.BlockSpec(memory_space=pltpu.VMEM),) * 2,
             scratch_shapes=[
                 pltpu.VMEM(block, f32),
@@ -427,9 +427,9 @@
             ],
             compiler_params=pltpu.CompilerParams(
                 collective_id=0, has_side_effects=True,
-                vmem_limit_bytes=60 * 1024 * 1024,
+                vmem_limit_bytes=16 * 1024 * 1024,
             ),
-        )(conductance, reaction, source)
+        )(*(pltpu.with_memory_space_constraint(a, pltpu.HBM) for a in (conductance, reaction, source)))
 
     placed = P("gx", "gy", "gz")
     return jax.shard_map(

time: 51.5 us -> 49.7 us (0.965)
  local copies, waits for them, and re-layouts: 2.42 us -> 1.41 us
  Pallas kernels: 48.3 us -> 47.5 us
    unnamed x4 -> x2, local copies, waits for them, and re-layouts: 2.42 us -> 1.41 us
    pallas_call x1, Pallas kernels: 48.3 us -> 47.5 us  [shards(): pl.pallas_call(functools.partial(kernel, sizes), out_shape=(jax.ShapeDtyp...]
where the time goes in v3:
time: 49.7 us; the launch traced here: 49.6 us
  Pallas kernels  47.5 us (96%)
  local copies, waits for them, and re-layouts  1.41 us (3%)
  between operations  0.64 us (1%)
    pallas_call x1, Pallas kernels, shards(): pl.pallas_call(functools.partial(kernel, sizes), out_shape=(jax.ShapeDtyp...  47.5 us
    unnamed x2, local copies, waits for them, and re-layouts  1.41 us

profile of v3, /device:TPU:0, one launch (start us, length us, event | category | flops | bytes accessed | tf_op | source)
XLA Modules:
  0.0 49.6 jit_solution(4283713174198986434)
XLA Ops:
  0.6 47.5 %shard_map.50 = (f32[16,32,128]{2,1,0:T(8,128)S(1)}, f32[16,32,128]{2,1,0:T(8,128)S(1)}) custom-call(f32[16,32,128]{2,1,0:T(8,128)} %cond_hbm.1, f32[16,32,128]{2,1,0:T(8,128)} %reac_hbm.1, f32[16,32,128]{2,1,0:T(8,128)} %src_hbm.1), custom_call_target="tpu_custom_call" | custom-call | tf_op jit(solution)/shard_map/pallas_call | solution.py:399
  48.2 0.7 %copy.7 = f32[16,32,128]{2,1,0:T(8,128)} copy(f32[16,32,128]{2,1,0:T(8,128)S(1)} %get-tuple-element.4) | data formatting | bytes 524288
  48.9 0.7 %copy.8 = f32[16,32,128]{2,1,0:T(8,128)} copy(f32[16,32,128]{2,1,0:T(8,128)S(1)} %get-tuple-element.5) | data formatting | bytes 524288

commit v4 on v3

--- a/solution.py
+++ b/solution.py
@@ -122,7 +122,6 @@
     barrier = pltpu.get_barrier_semaphore()
     for offset in everyone:
         pl.semaphore_signal(barrier, inc=1, device_id=at_offset(offset), device_id_type=MESH)
-    pl.semaphore_wait(barrier, len(everyone))
 
     def face_copy(e, axis, up):
         side = 0 if up else 1
@@ -224,9 +223,10 @@
     packs = blank()
     for x in order:
         emit(0, x, cond[x], packs)
-        if x == bx - 1:
-            send(0, 0)
-    finish(0, packs)
+    stage_z[0] = merge(packs)
+    pl.semaphore_wait(barrier, len(everyone))
+    for axis in (0, 2, 1):
+        send(0, axis)
     loads[1].wait()
     loads[2].wait()
     receive(0)
@@ -325,16 +325,22 @@
         receive(e)
         packed = edge_z[...] * edge_lanes(e)
         packs = blank()
+        odd = None
         for x in order:
             rest = zs[k + 1, x] + outer(e, x, packed)
             zs[k + 1, x] = rest
+            if last:
+                term = diag[x] * fields[e, x] * rest
+                odd = term if odd is None else odd + term
             if not last:
                 emit(e + 1, x, rest * first_scale, packs)
                 if x == bx - 1:
                     send(e + 1, 0)
         if not last:
             finish(e + 1, packs)
-        moment(k, k + 1)
+            moment(k, k + 1)
+        else:
+            hacc[pl.ds(2 * k + 1, 1), :] = jnp.sum(odd, axis=0, keepdims=True)
 
     hacc[...] = jnp.zeros_like(hacc)
 

time: 49.7 us -> 49.7 us (level)
  no operation moved by 1% of the time
where the time goes in v4:
time: 49.7 us; the launch traced here: 49.6 us
  Pallas kernels  47.5 us (96%)
  local copies, waits for them, and re-layouts  1.41 us (3%)
  between operations  0.64 us (1%)
    pallas_call x1, Pallas kernels, shards(): pl.pallas_call(functools.partial(kernel, sizes), out_shape=(jax.ShapeDtyp...  47.5 us
    unnamed x2, local copies, waits for them, and re-layouts  1.41 us

profile of v4, /device:TPU:0, one launch (start us, length us, event | category | flops | bytes accessed | tf_op | source)
XLA Modules:
  0.0 49.6 jit_solution(12760511126807849148)
XLA Ops:
  0.6 47.5 %shard_map.50 = (f32[16,32,128]{2,1,0:T(8,128)S(1)}, f32[16,32,128]{2,1,0:T(8,128)S(1)}) custom-call(f32[16,32,128]{2,1,0:T(8,128)} %cond_hbm.1, f32[16,32,128]{2,1,0:T(8,128)} %reac_hbm.1, f32[16,32,128]{2,1,0:T(8,128)} %src_hbm.1), custom_call_target="tpu_custom_call" | custom-call | tf_op jit(solution)/shard_map/pallas_call | solution.py:405
  48.1 0.7 %copy.7 = f32[16,32,128]{2,1,0:T(8,128)} copy(f32[16,32,128]{2,1,0:T(8,128)S(1)} %get-tuple-element.4) | data formatting | bytes 524288
  48.9 0.7 %copy.8 = f32[16,32,128]{2,1,0:T(8,128)} copy(f32[16,32,128]{2,1,0:T(8,128)S(1)} %get-tuple-element.5) | data formatting | bytes 524288
